TPU v7x, 32 devices: a whole 2x2x4 slice. The times are simulated.
32 devices in a mesh: blk: 8 (over y, x, core), ulysses: 4 (over z).
Axes of the slice: x: 2, y: 2, z: 4, core: 2. Of those that a mesh axis runs over, the one named last changes fastest.
Arguments:
- queries: bfloat16 [4096, 2048], P(('blk', 'ulysses')), may hold values from -6 to 6
- key_states: bfloat16 [4096, 512], P(('blk', 'ulysses')), may hold values from -6 to 6
- value_states: bfloat16 [4096, 512], P(('blk', 'ulysses')), may hold values from -6 to 6
- attn_out: bfloat16 [4096, 2048], P(('blk', 'ulysses')), may hold values from -6 to 6
- grad_out: bfloat16 [4096, 2048], P(('blk', 'ulysses')), may hold values from -6 to 6
- log_sums: float32 [4096, 32], P(('blk', 'ulysses')), may hold values from 2 to 4
- owners: int32 [16], replicated, may hold values from 0 to 15, as said below
Outputs:
- grad_query: bfloat16 [4096, 2048], P(('blk', 'ulysses'))
- grad_key: bfloat16 [4096, 512], P(('blk', 'ulysses'))
- grad_value: bfloat16 [4096, 512], P(('blk', 'ulysses'))
Inputs may be any that keep to these rules, and one draw needn't show every extreme that they name: `owners`: every value 0 to 15 appears exactly once; each sequence block holds one half-block below 8 and the half-block 2 * 8 - 1 minus it.
All inputs are finite; a program needn't handle non-finite values.
Results may differ from a plain program's by a relative error of at most 0.0049.
Values may be sent and summed in bfloat16 or wider, within the bound.
No kernel may reach another device: no remote copies, remote signals or barrier semaphores. Data moves between devices by JAX's collectives and lax.ppermute only.
A program may use at most 64 MiB of HBM per device.

v0:
```python
import functools
import math

import jax
import jax.numpy as jnp
from jax import lax
from jax.experimental import pallas as pl
from jax.experimental.pallas import tpu as pltpu
from jax.sharding import PartitionSpec as P

HEAD_DIM = 64
LANES = 128
PACK_MIB = 60
TURNS_MIB = 53.4
NONE, SHORT, OWN, PARTNER, LONG = 1 << 20, 7 << 27, 1 << 31, 1 << 31, 1 << 34
LOG2E = math.log2(math.e)
BF16 = jnp.bfloat16
F32 = jnp.float32
ANY = pl.BlockSpec(memory_space=pl.ANY)
VMEM = pl.BlockSpec(memory_space=pltpu.VMEM)
SMEM = pl.BlockSpec(memory_space=pltpu.SMEM)


def dot(a, b, a_dim, b_dim):
    return lax.dot_general(
        a, b, (((a_dim,), (b_dim,)), ((), ())), preferred_element_type=F32
    )


def parity():
    return lax.rem(lax.axis_index("ulysses"), 2)


def by_parity(write):
    for mine in range(2):

        @pl.when(parity() == mine)
        def _():
            write(mine, 1 - mine)


def by_class(write):
    side = lax.div(lax.axis_index("ulysses"), lax.axis_size("ulysses") // 2)
    odd = lax.rem(lax.axis_index("blk") + side, 2)
    for which in range(2):

        @pl.when(odd == which)
        def _():
            write(which)


def in_turn(which, first, second):
    return [*first, *second] if which == 0 else [*second, *first]


def apart(which, refs, n_first):
    n_second = len(refs) - n_first
    if which == 0:
        return refs[:n_first], refs[n_first:]
    return refs[n_second:], refs[:n_second]


def cut(ref, which, size, at=0, wide=None):
    wide = size if wide is None else wide
    return ref[:, pl.ds(pl.multiple_of(which * size + at, wide), wide)]


def put_keys(out, k, v, which):
    part = k.shape[1] // 2
    out[:, :part] = cut(k, which, part)
    out[:, part:] = cut(v, which, part)


def put_rows(out, q, do, part, unit, at=0):
    half = q.shape[1] // 2
    other = 1 - parity()
    out[:, at : at + part] = cut(q, other, half, unit * part, part)
    out[:, at + part : at + 2 * part] = cut(do, other, half, unit * part, part)


def pack_turns_kernel(side, q, do, k, v, *slots):
    *slots, ready = slots
    ready[...] = jnp.zeros_like(ready)
    mine = parity()

    def write(which):
        keys, rows = apart(which, slots, side)
        for d in range(side):
            put_keys(keys[d], k, v, mine if d % 2 == 0 else 1 - mine)
        for unit in range(len(rows)):
            put_rows(rows[unit], q, do, k.shape[1] // 2, unit)

    by_class(write)


def pack_kernel(n_mixed, q, do, o, sums, k, v, _, near_same, near_other, rest, stat_own):
    tokens, width = do.shape
    heads = sums.shape[0]
    part = k.shape[1] // 2
    n = heads // 2
    put_keys(near_same, k, v, parity())
    put_keys(near_other, k, v, 1 - parity())
    for unit in range(n_mixed, width // 2 // part):
        put_rows(rest, q, do, part, unit, (unit - n_mixed) * 2 * part)

    row = lax.broadcasted_iota(jnp.int32, (heads, width), 0)
    col = lax.broadcasted_iota(jnp.int32, (heads, width), 1)
    pick = jnp.where(col // HEAD_DIM == row, 1.0, 0.0).astype(BF16)
    prod = do[...].astype(F32) * o[...].astype(F32)
    high = prod.astype(BF16)
    low = (prod - high.astype(F32)).astype(BF16)
    delta = dot(pick, high, 1, 1) + dot(pick, low, 1, 1)
    lse = sums[...] * LOG2E

    def write_stats(mine, other):
        stat_own[:n, :] = lse[mine * n : (mine + 1) * n, :]
        stat_own[n:, :] = delta[mine * n : (mine + 1) * n, :]
        left = jnp.concatenate([x[other * n : (other + 1) * n, :] for x in (lse, delta)], 0)
        terms = []
        for _ in range(3):
            term = left.astype(BF16).astype(F32)
            left = left - term
            terms.append(term)
        terms.append(jnp.zeros((LANES - 6 * n, tokens), F32))
        rest[:, rest.shape[1] - LANES :] = jnp.transpose(jnp.concatenate(terms, 0)).astype(BF16)

    by_parity(write_stats)


def stack_heads(load, first, group):
    blocks = []
    for pair in range(group // 2):
        two = load((first + 2 * pair) * HEAD_DIM, 2 * HEAD_DIM)
        blocks += [two[:, :HEAD_DIM], two[:, HEAD_DIM:]]
    return jnp.concatenate(blocks, 0)


def stack_stats(stats, first, group):
    return jnp.concatenate([stats[first + g : first + g + 1] for g in range(group)], 1)


def head_grads(q, do, lse, delta, k, v):
    scores = dot(k, q, 1, 1)
    dprobs = dot(v, do, 1, 1)
    probs = jnp.exp2(scores * (LOG2E / math.sqrt(HEAD_DIM)) - lse)
    dscores = (probs * (dprobs - delta)).astype(BF16)
    dv = dot(probs.astype(BF16), do, 1, 0)
    dk = dot(dscores, q, 1, 0)
    dq = dot(k, dscores, 0, 0)
    return dk, dv, dq


def side_grads(pairs, load_q, load_do, load_stats, kv, put):
    part = kv.shape[1] // 2
    width = 2 * HEAD_DIM
    for pair in pairs:
        at = pair * width
        k_two, v_two = kv[:, at : at + width], kv[:, part + at : part + at + width]
        dks, dvs = [], []
        for odd in range(2):
            first = (2 * pair + odd) * put.group
            lanes = slice(odd * HEAD_DIM, (odd + 1) * HEAD_DIM)
            dk, dv, dq = head_grads(
                stack_heads(load_q, first, put.group),
                stack_heads(load_do, first, put.group),
                *load_stats(first),
                k_two[:, lanes],
                v_two[:, lanes],
            )
            dks.append(dk)
            dvs.append(dv)
            put(first, dq)
        put.store(at, jnp.concatenate(dks, 1), jnp.concatenate(dvs, 1))


class Put:
    def __init__(self, dq_acc, group, store):
        self.dq_acc, self.group, self.store = dq_acc, group, store

    def __call__(self, first, dq):
        tok = self.dq_acc.shape[1]
        for g in range(self.group):
            rows = slice((first + g) * HEAD_DIM, (first + g + 1) * HEAD_DIM)
            self.dq_acc[rows, :] += dq[:, g * tok : (g + 1) * tok]


def turned_dq(dq_acc, first, last):
    factor = 1.0 / math.sqrt(HEAD_DIM)
    blocks = [
        jnp.transpose(dq_acc[at : at + LANES, :])
        for at in range(first * HEAD_DIM, last * HEAD_DIM, LANES)
    ]
    return (jnp.concatenate(blocks, 1) * factor).astype(BF16)


def seen(flags, which):
    return jnp.max(flags[which : which + 1, :]) > 0


def seen_sides(owners, shards):
    rank, z = lax.axis_index("blk"), lax.axis_index("ulysses")
    n_blk = lax.axis_size("blk")
    before = lax.rem(rank + n_blk - 1, n_blk)
    place = lax.div(z, shards // 2)
    mine = owners[2 * rank + place]
    return mine > owners[2 * before + place], mine > owners[2 * before + 1 - place]


def own_loaders(q, do, stats, group):
    heads = stats.shape[0] // 2
    half = heads * HEAD_DIM
    mine = parity()

    def from_half(ref):
        def load(at, size):
            return ref[:, pl.ds(pl.multiple_of(mine * half + at, size), size)]

        return load

    def load_stats(first):
        every = stats[...]
        return stack_stats(every, first, group), stack_stats(every, heads + first, group)

    return from_half(q), from_half(do), load_stats


def partner_loaders(q_in, rest, part, heads):
    tok, kv_width = rest.shape[0], 2 * part
    n_mixed = q_in.shape[0] // tok

    def loader(offset):
        def load(at, size):
            unit, lane = at // part, offset + at % part
            if unit < n_mixed:
                return q_in[unit * tok : (unit + 1) * tok, lane : lane + size]
            lane += (unit - n_mixed) * kv_width
            return rest[:, lane : lane + size]

        return load

    def load_stats(first):
        terms = jnp.transpose(rest[:, rest.shape[1] - LANES :].astype(F32))
        n = 2 * heads
        every = terms[:n] + terms[n : 2 * n] + terms[2 * n : 3 * n]
        group = part // HEAD_DIM
        return stack_stats(every, first, group), stack_stats(every, heads + first, group)

    return loader(0), loader(part), load_stats


def finish(outs, acc, at, dk, dv):
    part, tok = acc.shape[1] // 2, outs[0].shape[0]
    dk = (dk + acc[:, at : at + LANES]) * (1.0 / math.sqrt(HEAD_DIM))
    dv = dv + acc[:, part + at : part + at + LANES]
    for d, out in enumerate(outs):
        rows = slice(d * tok, (d + 1) * tok)
        out[:, at : at + LANES] = dk[rows].astype(BF16)
        out[:, part + at : part + at + LANES] = dv[rows].astype(BF16)


def own_far_kernel(side, owners, q, do, stats, *rest):
    slots = rest[:-5]
    kv, q_in, acc, dq_acc, flags = rest[-5:]
    near_seen, far_seen = seen_sides(owners, 2 * side)
    line = lax.broadcasted_iota(jnp.int32, flags.shape, 0)
    flags[...] = jnp.where(line == 0, near_seen.astype(jnp.int32), far_seen.astype(jnp.int32))
    tok, part = q.shape[0], kv.shape[1] // 2

    def sort(which):
        keys, rows = apart(which, slots, side)
        for d in range(side):
            kv[d * tok : (d + 1) * tok, :] = keys[d][...]
        for unit in range(len(rows)):
            q_in[unit * tok : (unit + 1) * tok, :] = rows[unit][...]

    by_class(sort)
    dq_acc[...] = jnp.zeros_like(dq_acc)

    def store(at, dk, dv):
        acc[:, at : at + LANES] = dk
        acc[:, part + at : part + at + LANES] = dv

    @pl.when(far_seen)
    def _():
        group = part // HEAD_DIM
        loaders = own_loaders(q, do, stats, group)
        side_grads(range(part // LANES), *loaders, kv, Put(dq_acc, group, store))


def partner_far_kernel(flags, q_in, rest, kv, acc, *outs):
    far, dq_acc = outs[:-1], outs[-1]
    tok, part = rest.shape[0], kv.shape[1] // 2
    dq_acc[...] = jnp.zeros_like(dq_acc)

    def store(at, dk, dv):
        finish(far, acc, at, dk, dv)

    @pl.when(seen(flags, 1))
    def _():
        loaders = partner_loaders(q_in, rest, part, dq_acc.shape[0] // HEAD_DIM)
        side_grads(range(part // LANES), *loaders, kv, Put(dq_acc, part // HEAD_DIM, store))

    @pl.when(jnp.logical_not(seen(flags, 1)))
    def _():
        for out in far:
            out[...] = jnp.zeros_like(out)


def partner_near_kernel(side, flags, q_in, rest, partner_dq, *refs):
    keys, refs = refs[:side], refs[side:]
    kv, acc, dq_acc = refs[-3:]
    tok, part = rest.shape[0], kv.shape[1] // 2
    heads = dq_acc.shape[0] // HEAD_DIM
    group = part // HEAD_DIM
    n_late = (len(refs) - 4) // 2
    far, far_out, dq_send = refs[:n_late], refs[n_late : 2 * n_late], refs[-4]
    dq_acc[...] = partner_dq[...]

    @pl.when(seen(flags, 0))
    def _():
        for d in range(side):
            kv[d * tok : (d + 1) * tok, :] = keys[d][...]

        def store(at, dk, dv):
            acc[:, at : at + LANES] = dk
            acc[:, part + at : part + at + LANES] = dv

        loaders = partner_loaders(q_in, rest, part, heads)
        side_grads(range(part // LANES), *loaders, kv, Put(dq_acc, group, store))

    for out, ref in zip(far_out, far):
        out[...] = ref[...]
    dq_send[...] = turned_dq(dq_acc, 0, heads)


def own_near_kernel(flags, q, do, stats, kv, acc, own_dq, *outs):
    *near, dq_own, dq_acc = outs
    part = kv.shape[1] // 2
    group = part // HEAD_DIM
    dq_acc[...] = own_dq[...]

    @pl.when(seen(flags, 0))
    def _():
        def store(at, dk, dv):
            finish(near, acc, at, dk, dv)

        loaders = own_loaders(q, do, stats, group)
        side_grads(range(part // LANES), *loaders, kv, Put(dq_acc, group, store))

    @pl.when(jnp.logical_not(seen(flags, 0)))
    def _():
        for out in near:
            out[...] = jnp.zeros_like(out)

    dq_own[...] = turned_dq(dq_acc, 0, dq_acc.shape[0] // HEAD_DIM)


def take_kernel(count, *refs):
    for ref, out in zip(refs[:count], refs[-count:]):
        out[...] = ref[...].astype(out.dtype)


def join_kernel(side, dq_own, *refs):
    far, dq_back, near = refs[:side], refs[side], refs[side + 1 : -3][::-1]
    gq, gk, gv = refs[-3:]
    half = dq_own.shape[1]
    part = gk.shape[1] // 2
    totals = []
    for odd in range(2):
        terms = [*near[odd::2], *far[odd::2]]
        totals.append(sum((ref[...].astype(F32) for ref in terms[1:]), terms[0][...].astype(F32)))

    def write(mine, other):
        gq[:, mine * half : (mine + 1) * half] = dq_own[...]
        gq[:, other * half : (other + 1) * half] = dq_back[...]
        for total, place in zip(totals, (mine, other)):
            gk[:, place * part : (place + 1) * part] = total[:, :part].astype(BF16)
            gv[:, place * part : (place + 1) * part] = total[:, part:].astype(BF16)

    by_parity(write)


def limit(mib):
    return pltpu.CompilerParams(vmem_limit_bytes=int(mib * 1024 * 1024))


def per_device(queries, key_states, value_states, attn_out, grad_out, log_sums, owners):
    n_blk, n_uly = lax.axis_size("blk"), lax.axis_size("ulysses")
    tok, width = queries.shape
    heads = log_sums.shape[1]
    kv_width = key_states.shape[1]
    half = width // 2
    side = n_uly // 2

    n_units = width // kv_width
    n_mixed = min(n_units, side)

    def flips(first, second):
        return [in_turn(which, first, second) for which in range(2)]

    def move(value, *by_kind):
        pairs = []
        for b in range(n_blk):
            for u in range(n_uly):
                step, flip = by_kind[(b + u // side) % len(by_kind)]
                pairs.append((b * n_uly + u, ((b + step) % n_blk) * n_uly + (u ^ flip)))
        return lax.ppermute(value, ("blk", "ulysses"), pairs)

    def shape(*dims, dtype=BF16):
        return jax.ShapeDtypeStruct(dims, dtype)

    def cover(flops):
        return pl.CostEstimate(flops=flops, bytes_accessed=1 << 20, transcendentals=0)

    unit = shape(tok, kv_width)
    sides = shape(side * tok, kv_width)
    sides_wide = shape(side * tok, kv_width, dtype=F32)
    dq_wide = shape(half, tok, dtype=F32)
    *slots, ready = pl.pallas_call(
        functools.partial(pack_turns_kernel, side),
        out_shape=[unit] * (side + n_mixed) + [shape(8, LANES, dtype=F32)],
        in_specs=[VMEM] * 4,
        out_specs=[VMEM] * (side + n_mixed + 1),
        compiler_params=limit(TURNS_MIB),
        name="pack_turns",
    )(queries, grad_out, key_states, value_states)
    near_same, near_other, rest, stat_own = pl.pallas_call(
        functools.partial(pack_kernel, n_mixed),
        out_shape=[unit] * 2
        + [
            shape(tok, (n_units - n_mixed) * kv_width + LANES),
            shape(heads, tok, dtype=F32),
        ],
        in_specs=[VMEM] * 6 + [ANY],
        out_specs=[VMEM] * 4,
        compiler_params=limit(PACK_MIB),
        name="pack",
    )(
        queries, grad_out, attn_out, jnp.transpose(log_sums), key_states, value_states, ready
    )
    turns = flips([(1, d) for d in range(side, n_uly)], [(0, 1)] * n_mixed)
    slots = [move(x, one, two) for x, one, two in zip(slots, *turns)]
    rest = move(rest, (0, 1))
    near = [move(near_other if d % 2 else near_same, (1, d)) for d in range(side)]
    outs = [sides, shape(n_mixed * tok, kv_width), sides_wide, dq_wide]
    outs.append(shape(8, LANES, dtype=jnp.int32))
    kv_far, q_in, acc_far, own_dq, flags = pl.pallas_call(
        functools.partial(own_far_kernel, side),
        out_shape=outs,
        in_specs=[SMEM] + [VMEM] * (3 + side + n_mixed),
        out_specs=[VMEM] * len(outs),
        compiler_params=limit(32),
        cost_estimate=cover(OWN),
        name="own_far",
    )(owners, queries, grad_out, stat_own, *slots)
    *far, partner_dq = pl.pallas_call(
        partner_far_kernel,
        out_shape=[unit] * side + [dq_wide],
        in_specs=[VMEM] * 5,
        out_specs=[VMEM] * (side + 1),
        compiler_params=limit(32),
        cost_estimate=cover(PARTNER),
        name="far",
    )(flags, q_in, rest, kv_far, acc_far)
    n_early = side // 2
    n_late = side - n_early
    early = [move(x, (-1, side + d)) for d, x in enumerate(far[:n_early])]
    outs = [unit] * n_late + [shape(tok, half), sides, sides_wide]
    *late, dq_back, kv_near, acc_near = pl.pallas_call(
        functools.partial(partner_near_kernel, side),
        out_shape=outs,
        in_specs=[VMEM] * (4 + side + n_late),
        out_specs=[VMEM] * len(outs),
        scratch_shapes=[pltpu.VMEM(dq_wide.shape, F32)],
        compiler_params=limit(32),
        cost_estimate=cover(PARTNER),
        name="near",
    )(flags, q_in, rest, partner_dq, *near, *far[n_early:])
    late = [move(x, (-1, side + n_early + d)) for d, x in enumerate(late)]
    dq_back = move(dq_back, (0, 1))
    outs = [unit] * side + [shape(tok, half)]
    *near, dq_own = pl.pallas_call(
        own_near_kernel,
        out_shape=outs,
        in_specs=[VMEM] * 7,
        out_specs=[VMEM] * len(outs),
        scratch_shapes=[pltpu.VMEM(dq_wide.shape, F32)],
        compiler_params=limit(32),
        cost_estimate=cover(NONE),
        name="own_near",
    )(flags, queries, grad_out, stat_own, kv_near, acc_near, own_dq)
    near = [move(near[d], (-1, d)) for d in reversed(range(side))][::-1]

    def take(first, outs, flops, *after):
        return pl.pallas_call(
            functools.partial(take_kernel, len(first)),
            out_shape=outs,
            in_specs=[VMEM] * len(first) + [ANY] * len(after),
            out_specs=[VMEM] * len(first),
            compiler_params=limit(8),
            cost_estimate=cover(flops),
            name="take",
        )(*first, *after)

    wide = shape(tok, kv_width, dtype=F32)
    early = take(early, [wide] * n_early, SHORT)
    late = take(late, [wide] * n_late, SHORT, early[0])
    (dq_back,) = take([dq_back], [shape(tok, half)], LONG, late[0])
    ins = [dq_own, *early, *late, dq_back, *near[::-1]]
    return tuple(
        pl.pallas_call(
            functools.partial(join_kernel, side),
            out_shape=[shape(tok, width), shape(tok, kv_width), shape(tok, kv_width)],
            in_specs=[VMEM] * len(ins),
            out_specs=[VMEM] * 3,
            compiler_params=limit(8),
            name="join",
        )(*ins)
    )


def solution(mesh):
    rows = P(("blk", "ulysses"), None)
    return jax.shard_map(
        per_device,
        mesh=mesh,
        in_specs=(rows, rows, rows, rows, rows, rows, P()),
        out_specs=(rows, rows, rows),
        check_vma=False,
    )
```

profile of v0, /device:TPU:1, one launch (start us, length us, event | category | flops | bytes accessed | tf_op | source)
XLA Modules:
  0.0 48.1 jit_solution(9470557593001875434)
XLA Ops:
  0.6 1.3 %pack_turns.1 = (bf16[128,512]{1,0:T(8,128)(2,1)S(1)}, bf16[128,512]{1,0:T(8,128)(2,1)S(1)}, bf16[128,512]{1,0:T(8,128)(2,1)S(1)}, bf16[128,512]{1,0:T(8,128)(2,1)S(1)}, f32[8,128]{1,0:T(8,128)S(1)}) custom-call(bf16[128,2048]{1,0:T(8,128)(2,1)} %q.7, bf16[128,2048]{1,0:T(8,128)(2,1)} %do.7, bf16[128,512]{1,0:T(8,128)(2,1)} %k.3, bf16[128,512]{1,0:T(8,128)(2,1)} %v.3), custom_call_target="tpu_custom_call" | custom-call | tf_op jit(solution)/shard_map/pack_turns/pallas_call | solution.py:419
  1.9 0.0 copy-start.3
  2.0 2.2 %collective-permute-start = (bf16[128,512]{1,0:T(8,128)(2,1)S(1)}, bf16[128,512]{1,0:T(8,128)(2,1)S(1)}, u32[]{:S(2)}, u32[]{:S(2)}) collective-permute-start(bf16[128,512]{1,0:T(8,128)(2,1)S(1)} %get-tuple-element.29), channel_id=1, source_target_pairs={{0,6},{1,7},{2,3},{3,2},{4,5},{5,4},{6,8},{7,9},{8,14},{9,15},{10,... | collective-permute-start | bytes 393224 | tf_op jit(solution)/shard_map/ppermute | solution.py:407
  4.1 0.1 collective-permute-start.1
  4.2 4.5 %collective-permute-start.2 = (bf16[128,512]{1,0:T(8,128)(2,1)S(1)}, bf16[128,512]{1,0:T(8,128)(2,1)S(1)}, u32[]{:S(2)}, u32[]{:S(2)}) collective-permute-start(bf16[128,512]{1,0:T(8,128)(2,1)S(1)} %get-tuple-element.31), channel_id=1, source_target_pairs={{0,1},{1,0},{2,4},{3,5},{4,10},{5,11},{6,7},{7,6},{8,9},{9,8},{10,... | collective-permute-start | bytes 393224 | tf_op jit(solution)/shard_map/ppermute | solution.py:407
  8.7 1.0 %collective-permute-start.3 = (bf16[128,512]{1,0:T(8,128)(2,1)S(1)}, bf16[128,512]{1,0:T(8,128)(2,1)S(1)}, u32[]{:S(2)}, u32[]{:S(2)}) collective-permute-start(bf16[128,512]{1,0:T(8,128)(2,1)S(1)} %get-tuple-element.32), channel_id=1, source_target_pairs={{0,1},{1,0},{2,5},{3,4},{4,11},{5,10},{6,7},{7,6},{8,9},{9,8},{10,... | collective-permute-start | bytes 393224 | tf_op jit(solution)/shard_map/ppermute | solution.py:407
  9.7 0.0 copy-done.3
  9.7 0.0 copy-start
  9.7 0.0 copy-start.1
  9.7 2.9 %pack.1 = (bf16[128,512]{1,0:T(8,128)(2,1)}, bf16[128,512]{1,0:T(8,128)(2,1)}, bf16[128,1152]{1,0:T(8,128)(2,1)}, f32[32,128]{1,0:T(8,128)}) custom-call(bf16[128,2048]{1,0:T(8,128)(2,1)} %q.7, bf16[128,2048]{1,0:T(8,128)(2,1)} %do.7, bf16[128,2048]{1,0:T(8,128)(2,1)} %o.1, f32[32,128]{1,0:T(8,128)} %bitcast.1, bf16[128,512]{1,0:T(8,128)(2,1)} %k.3, ...), custom_call_target="tpu_custom_call" | custom-call | tf_op jit(solution)/shard_map/pack/pallas_call | solution.py:427
  12.6 0.3 collective-permute-start.4
  12.9 0.0 collective-permute-done.rest_0_
  12.9 1.3 %collective-permute-start.5 = (bf16[128,512]{1,0:T(8,128)(2,1)}, bf16[128,512]{1,0:T(8,128)(2,1)S(1)}, u32[]{:S(2)}, u32[]{:S(2)}) collective-permute-start(bf16[128,512]{1,0:T(8,128)(2,1)} %get-tuple-element.39), channel_id=1, source_target_pairs={{0,4},{1,5},{2,6},{3,7},{4,8},{5,9},{6,10},{7,11},{8,12},{9,13},{1... | collective-permute-start | bytes 393224 | tf_op jit(solution)/shard_map/ppermute | solution.py:407
  14.2 0.0 collective-permute-done.1.rest_1_
  14.2 0.0 copy-start.4
  14.2 4.5 %collective-permute-start.6 = (bf16[128,512]{1,0:T(8,128)(2,1)}, bf16[128,512]{1,0:T(8,128)(2,1)S(1)}, u32[]{:S(2)}, u32[]{:S(2)}) collective-permute-start(bf16[128,512]{1,0:T(8,128)(2,1)} %get-tuple-element.40), channel_id=1, source_target_pairs={{0,5},{1,4},{2,7},{3,6},{4,9},{5,8},{6,11},{7,10},{8,13},{9,12},{1... | collective-permute-start | bytes 393224 | tf_op jit(solution)/shard_map/ppermute | solution.py:407
  18.7 0.0 collective-permute-done.2.rest_2_
  18.7 0.7 %collective-permute-done.3.rest_3_ = bf16[128,512]{1,0:T(8,128)(2,1)S(1)} collective-permute-done((bf16[128,512]{1,0:T(8,128)(2,1)S(1)}, bf16[128,512]{1,0:T(8,128)(2,1)S(1)}, u32[]{:S(2)}, u32[]{:S(2)}) %collective-permute-start.3) | collective-permute-done | bytes 131104 | tf_op jit(solution)/shard_map/ppermute | solution.py:407
  19.4 0.0 copy-done
  19.4 0.0 copy-done.1
  19.4 0.0 copy-done.4
  19.4 0.0 copy-start.2
  19.4 0.7 %copy-done.2 = f32[32,128]{1,0:T(8,128)S(1)} copy-done((f32[32,128]{1,0:T(8,128)S(1)}, f32[32,128]{1,0:T(8,128)}, u32[]{:S(2)}) %copy-start.2) | copy-done | bytes 16408
  20.1 0.6 %own_far.1 = (bf16[256,512]{1,0:T(8,128)(2,1)S(1)}, bf16[256,512]{1,0:T(8,128)(2,1)S(1)}, f32[256,512]{1,0:T(8,128)S(1)}, f32[1024,128]{1,0:T(8,128)S(1)}, s32[8,128]{1,0:T(8,128)S(1)}) custom-call(s32[16]{0:T(128)S(1)} %copy-done.4, bf16[128,2048]{1,0:T(8,128)(2,1)S(1)} %copy-done, bf16[128,2048]{1,0:T(8,128)(2,1)S(1)} %copy-done.1, ...), custom_call_target="tpu_custom_call" | custom-call | flops 2147483648 | bytes 1048576 | tf_op jit(solution)/shard_map/own_far/pallas_call | solution.py:447
  20.8 2.5 %collective-permute-done.4.rest = bf16[128,1152]{1,0:T(8,128)(2,1)S(1)} collective-permute-done((bf16[128,1152]{1,0:T(8,128)(2,1)}, bf16[128,1152]{1,0:T(8,128)(2,1)S(1)}, u32[]{:S(2)}, u32[]{:S(2)}) %collective-permute-start.4) | collective-permute-done | bytes 294944 | tf_op jit(solution)/shard_map/ppermute | solution.py:407
  23.3 0.4 far.1
  23.7 3.4 %collective-permute-start.7 = (bf16[128,512]{1,0:T(8,128)(2,1)S(1)}, bf16[128,512]{1,0:T(8,128)(2,1)S(1)}, u32[]{:S(2)}, u32[]{:S(2)}) collective-permute-start(bf16[128,512]{1,0:T(8,128)(2,1)S(1)} %get-tuple-element.46), channel_id=1, source_target_pairs={{0,30},{1,31},{2,28},{3,29},{4,2},{5,3},{6,0},{7,1},{8,6},{9,7},{1... | collective-permute-start | bytes 393224 | tf_op jit(solution)/shard_map/ppermute | solution.py:407
  27.1 0.0 collective-permute-done.5.refs_0_
  27.1 0.0 collective-permute-done.6.refs_1_
  27.1 0.4 near.1
  27.5 0.3 collective-permute-start.9
  27.7 7.0 %collective-permute-start.8 = (bf16[128,512]{1,0:T(8,128)(2,1)S(1)}, bf16[128,512]{1,0:T(8,128)(2,1)S(1)}, u32[]{:S(2)}, u32[]{:S(2)}) collective-permute-start(bf16[128,512]{1,0:T(8,128)(2,1)S(1)} %get-tuple-element.47), channel_id=1, source_target_pairs={{0,31},{1,30},{2,29},{3,28},{4,3},{5,2},{6,1},{7,0},{8,7},{9,6},{1... | collective-permute-start | bytes 393224 | tf_op jit(solution)/shard_map/ppermute | solution.py:407
  34.7 0.6 %own_near.1 = (bf16[128,512]{1,0:T(8,128)(2,1)S(1)}, bf16[128,512]{1,0:T(8,128)(2,1)S(1)}, bf16[128,1024]{1,0:T(8,128)(2,1)S(1)}) custom-call(s32[8,128]{1,0:T(8,128)S(1)} %get-tuple-element.33.flags, bf16[128,2048]{1,0:T(8,128)(2,1)S(1)} %copy-done, bf16[128,2048]{1,0:T(8,128)(2,1)S(1)} %copy-done.1, f32[32,128]{1,0:T(8,128)S(1)} %copy-done.2, ...), custom_call_target="tpu_custom_call" | custom-call | flops 1048576 | bytes 1048576 | tf_op jit(solution)/shard_map/own_near/pallas_call | solution.py:482
  35.3 0.1 collective-permute-start.10
  35.4 2.7 %collective-permute-start.11 = (bf16[128,512]{1,0:T(8,128)(2,1)S(1)}, bf16[128,512]{1,0:T(8,128)(2,1)S(1)}, u32[]{:S(2)}, u32[]{:S(2)}) collective-permute-start(bf16[128,512]{1,0:T(8,128)(2,1)S(1)} %get-tuple-element.50), channel_id=1, source_target_pairs={{0,28},{1,29},{2,30},{3,31},{4,0},{5,1},{6,2},{7,3},{8,4},{9,5},{1... | collective-permute-start | bytes 393224 | tf_op jit(solution)/shard_map/ppermute | solution.py:407
  38.1 0.0 collective-permute-done.7.refs_0_
  38.1 4.1 %collective-permute-done.8.refs_0_ = bf16[128,512]{1,0:T(8,128)(2,1)S(1)} collective-permute-done((bf16[128,512]{1,0:T(8,128)(2,1)S(1)}, bf16[128,512]{1,0:T(8,128)(2,1)S(1)}, u32[]{:S(2)}, u32[]{:S(2)}) %collective-permute-start.8) | collective-permute-done | bytes 131104 | tf_op jit(solution)/shard_map/ppermute | solution.py:407
  42.2 0.0 collective-permute-done.9.refs_0_
  42.3 4.8 %collective-permute-done.10.refs_3_ = bf16[128,512]{1,0:T(8,128)(2,1)S(1)} collective-permute-done((bf16[128,512]{1,0:T(8,128)(2,1)S(1)}, bf16[128,512]{1,0:T(8,128)(2,1)S(1)}, u32[]{:S(2)}, u32[]{:S(2)}) %collective-permute-start.10) | collective-permute-done | bytes 131104 | tf_op jit(solution)/shard_map/ppermute | solution.py:407
  47.1 0.0 collective-permute-done.11.refs_4_
  47.1 1.0 %join.1 = (bf16[128,2048]{1,0:T(8,128)(2,1)}, bf16[128,512]{1,0:T(8,128)(2,1)}, bf16[128,512]{1,0:T(8,128)(2,1)}) custom-call(bf16[128,1024]{1,0:T(8,128)(2,1)S(1)} %get-tuple-element.45.dq_own, f32[128,512]{1,0:T(8,128)S(1)} %take.3.refs_1_.refs_0_, f32[128,512]{1,0:T(8,128)S(1)} %take.4.refs_1_, bf16[128,1024]{1,0:T(8,128)(2,1)S(1)} %take.5.refs_2_, ...), custom_call_target="tpu_custom_call" | custom-call | tf_op jit(solution)/shard_map/join/pallas_call | solution.py:511
  (3 shorter events, 0.1 us)
Async XLA Ops:
  1.9 7.7 %copy-start.3 = (f32[8,128]{1,0:T(8,128)}, f32[8,128]{1,0:T(8,128)S(1)}, u32[]{:S(2)}) copy-start(f32[8,128]{1,0:T(8,128)S(1)} %get-tuple-element.27._) | copy-start | bytes 12292
  2.0 10.9 %collective-permute-start = (bf16[128,512]{1,0:T(8,128)(2,1)S(1)}, bf16[128,512]{1,0:T(8,128)(2,1)S(1)}, u32[]{:S(2)}, u32[]{:S(2)}) collective-permute-start(bf16[128,512]{1,0:T(8,128)(2,1)S(1)} %get-tuple-element.29), channel_id=1, source_target_pairs={{0,6},{1,7},{2,3},{3,2},{4,5},{5,4},{6,8},{7,9},{8,14},{9,15},{10,... | collective-permute-start | bytes 393224 | tf_op jit(solution)/shard_map/ppermute | solution.py:407
  4.1 10.0 %collective-permute-start.1 = (bf16[128,512]{1,0:T(8,128)(2,1)S(1)}, bf16[128,512]{1,0:T(8,128)(2,1)S(1)}, u32[]{:S(2)}, u32[]{:S(2)}) collective-permute-start(bf16[128,512]{1,0:T(8,128)(2,1)S(1)} %get-tuple-element.30), channel_id=1, source_target_pairs={{0,7},{1,6},{2,3},{3,2},{4,5},{5,4},{6,9},{7,8},{8,15},{9,14},{10,... | collective-permute-start | bytes 393224 | tf_op jit(solution)/shard_map/ppermute | solution.py:407
  4.2 14.5 %collective-permute-start.2 = (bf16[128,512]{1,0:T(8,128)(2,1)S(1)}, bf16[128,512]{1,0:T(8,128)(2,1)S(1)}, u32[]{:S(2)}, u32[]{:S(2)}) collective-permute-start(bf16[128,512]{1,0:T(8,128)(2,1)S(1)} %get-tuple-element.31), channel_id=1, source_target_pairs={{0,1},{1,0},{2,4},{3,5},{4,10},{5,11},{6,7},{7,6},{8,9},{9,8},{10,... | collective-permute-start | bytes 393224 | tf_op jit(solution)/shard_map/ppermute | solution.py:407
  8.7 10.7 %collective-permute-start.3 = (bf16[128,512]{1,0:T(8,128)(2,1)S(1)}, bf16[128,512]{1,0:T(8,128)(2,1)S(1)}, u32[]{:S(2)}, u32[]{:S(2)}) collective-permute-start(bf16[128,512]{1,0:T(8,128)(2,1)S(1)} %get-tuple-element.32), channel_id=1, source_target_pairs={{0,1},{1,0},{2,5},{3,4},{4,11},{5,10},{6,7},{7,6},{8,9},{9,8},{10,... | collective-permute-start | bytes 393224 | tf_op jit(solution)/shard_map/ppermute | solution.py:407
  9.7 9.7 %copy-start = (bf16[128,2048]{1,0:T(8,128)(2,1)S(1)}, bf16[128,2048]{1,0:T(8,128)(2,1)}, u32[]{:S(2)}) copy-start(bf16[128,2048]{1,0:T(8,128)(2,1)} %q.7) | copy-start | bytes 1572868
  9.7 9.7 %copy-start.1 = (bf16[128,2048]{1,0:T(8,128)(2,1)S(1)}, bf16[128,2048]{1,0:T(8,128)(2,1)}, u32[]{:S(2)}) copy-start(bf16[128,2048]{1,0:T(8,128)(2,1)} %do.7) | copy-start | bytes 1572868
  12.6 10.7 %collective-permute-start.4 = (bf16[128,1152]{1,0:T(8,128)(2,1)}, bf16[128,1152]{1,0:T(8,128)(2,1)S(1)}, u32[]{:S(2)}, u32[]{:S(2)}) collective-permute-start(bf16[128,1152]{1,0:T(8,128)(2,1)} %get-tuple-element.35), channel_id=1, source_target_pairs={{0,1},{1,0},{2,3},{3,2},{4,5},{5,4},{6,7},{7,6},{8,9},{9,8},{10,11... | collective-permute-start | bytes 884744 | tf_op jit(solution)/shard_map/ppermute | solution.py:407
  12.9 14.2 %collective-permute-start.5 = (bf16[128,512]{1,0:T(8,128)(2,1)}, bf16[128,512]{1,0:T(8,128)(2,1)S(1)}, u32[]{:S(2)}, u32[]{:S(2)}) collective-permute-start(bf16[128,512]{1,0:T(8,128)(2,1)} %get-tuple-element.39), channel_id=1, source_target_pairs={{0,4},{1,5},{2,6},{3,7},{4,8},{5,9},{6,10},{7,11},{8,12},{9,13},{1... | collective-permute-start | bytes 393224 | tf_op jit(solution)/shard_map/ppermute | solution.py:407
  14.2 5.2 %copy-start.4 = (s32[16]{0:T(128)S(1)}, s32[16]{0:T(128)}, u32[]{:S(2)}) copy-start(s32[16]{0:T(128)} %owners.1) | copy-start | bytes 196
  14.2 12.9 %collective-permute-start.6 = (bf16[128,512]{1,0:T(8,128)(2,1)}, bf16[128,512]{1,0:T(8,128)(2,1)S(1)}, u32[]{:S(2)}, u32[]{:S(2)}) collective-permute-start(bf16[128,512]{1,0:T(8,128)(2,1)} %get-tuple-element.40), channel_id=1, source_target_pairs={{0,5},{1,4},{2,7},{3,6},{4,9},{5,8},{6,11},{7,10},{8,13},{9,12},{1... | collective-permute-start | bytes 393224 | tf_op jit(solution)/shard_map/ppermute | solution.py:407
  19.4 0.7 %copy-start.2 = (f32[32,128]{1,0:T(8,128)S(1)}, f32[32,128]{1,0:T(8,128)}, u32[]{:S(2)}) copy-start(f32[32,128]{1,0:T(8,128)} %get-tuple-element.28.stats) | copy-start | bytes 49156
  23.7 14.4 %collective-permute-start.7 = (bf16[128,512]{1,0:T(8,128)(2,1)S(1)}, bf16[128,512]{1,0:T(8,128)(2,1)S(1)}, u32[]{:S(2)}, u32[]{:S(2)}) collective-permute-start(bf16[128,512]{1,0:T(8,128)(2,1)S(1)} %get-tuple-element.46), channel_id=1, source_target_pairs={{0,30},{1,31},{2,28},{3,29},{4,2},{5,3},{6,0},{7,1},{8,6},{9,7},{1... | collective-permute-start | bytes 393224 | tf_op jit(solution)/shard_map/ppermute | solution.py:407
  27.5 14.8 %collective-permute-start.9 = (bf16[128,1024]{1,0:T(8,128)(2,1)S(1)}, bf16[128,1024]{1,0:T(8,128)(2,1)S(1)}, u32[]{:S(2)}, u32[]{:S(2)}) collective-permute-start(bf16[128,1024]{1,0:T(8,128)(2,1)S(1)} %get-tuple-element.48), channel_id=1, source_target_pairs={{0,1},{1,0},{2,3},{3,2},{4,5},{5,4},{6,7},{7,6},{8,9},{9,8},{10,11... | collective-permute-start | bytes 786440 | tf_op jit(solution)/shard_map/ppermute | solution.py:407
  27.7 14.5 %collective-permute-start.8 = (bf16[128,512]{1,0:T(8,128)(2,1)S(1)}, bf16[128,512]{1,0:T(8,128)(2,1)S(1)}, u32[]{:S(2)}, u32[]{:S(2)}) collective-permute-start(bf16[128,512]{1,0:T(8,128)(2,1)S(1)} %get-tuple-element.47), channel_id=1, source_target_pairs={{0,31},{1,30},{2,29},{3,28},{4,3},{5,2},{6,1},{7,0},{8,7},{9,6},{1... | collective-permute-start | bytes 393224 | tf_op jit(solution)/shard_map/ppermute | solution.py:407
  35.3 11.8 %collective-permute-start.10 = (bf16[128,512]{1,0:T(8,128)(2,1)S(1)}, bf16[128,512]{1,0:T(8,128)(2,1)S(1)}, u32[]{:S(2)}, u32[]{:S(2)}) collective-permute-start(bf16[128,512]{1,0:T(8,128)(2,1)S(1)} %get-tuple-element.49), channel_id=1, source_target_pairs={{0,29},{1,28},{2,31},{3,30},{4,1},{5,0},{6,3},{7,2},{8,5},{9,4},{1... | collective-permute-start | bytes 393224 | tf_op jit(solution)/shard_map/ppermute | solution.py:407
  35.4 11.7 %collective-permute-start.11 = (bf16[128,512]{1,0:T(8,128)(2,1)S(1)}, bf16[128,512]{1,0:T(8,128)(2,1)S(1)}, u32[]{:S(2)}, u32[]{:S(2)}) collective-permute-start(bf16[128,512]{1,0:T(8,128)(2,1)S(1)} %get-tuple-element.50), channel_id=1, source_target_pairs={{0,28},{1,29},{2,30},{3,31},{4,0},{5,1},{6,2},{7,3},{8,4},{9,5},{1... | collective-permute-start | bytes 393224 | tf_op jit(solution)/shard_map/ppermute | solution.py:407
where the time goes:
time: 47.7 us; the launch traced here: 48.1 us
  starting transfers between devices  27.2 us (57%)
  waiting for transfers between devices  12.2 us (26%)
  Pallas kernels  7.28 us (15%)
  local copies, waits for them, and re-layouts  0.73 us (2%)
  between operations  0.73 us (2%)
    ppermute x12, starting transfers between devices, move(): return lax.ppermute(value, ('blk', 'ulysses'), pairs)  27.2 us
    ppermute x12, waiting for transfers between devices, move(): return lax.ppermute(value, ('blk', 'ulysses'), pairs)  12.2 us
    pallas_call x1, Pallas kernels, per_device(): pl.pallas_call(functools.partial(pack_kernel, n_mixed), out_shape=[unit]...  2.88 us
    pallas_call x1, Pallas kernels, per_device(): pl.pallas_call(functools.partial(pack_turns_kernel, side), out_shape=[uni...  1.32 us
    pallas_call x1, Pallas kernels, per_device(): pl.pallas_call(functools.partial(join_kernel, side), out_shape=[shape(tok...  0.97 us
  transfers between devices with their start and end apart: 12, of which 4 were waited for; matrix products, arithmetic and copies ran while one was open for 0% of the time, Pallas kernels for 10%

commit v1 on v0

--- a/solution.py
+++ b/solution.py
@@ -144,8 +144,8 @@
     dprobs = dot(v, do, 1, 1)
     probs = jnp.exp2(scores * (LOG2E / math.sqrt(HEAD_DIM)) - lse)
     dscores = (probs * (dprobs - delta)).astype(BF16)
-    dv = dot(probs.astype(BF16), do, 1, 0)
-    dk = dot(dscores, q, 1, 0)
+    dv = dot(do, probs.astype(BF16), 0, 1)
+    dk = dot(q, dscores, 0, 1)
     dq = dot(k, dscores, 0, 0)
     return dk, dv, dq
 
@@ -170,7 +170,7 @@
             dks.append(dk)
             dvs.append(dv)
             put(first, dq)
-        put.store(at, jnp.concatenate(dks, 1), jnp.concatenate(dvs, 1))
+        put.store(at, *(jnp.transpose(jnp.concatenate(x, 0)) for x in (dks, dvs)))
 
 
 class Put:

time: 47.7 us -> 47.5 us (level)
  starting transfers between devices: 27.2 us -> 26.7 us
    ppermute x12, starting transfers between devices: 27.2 us -> 26.7 us  [move(): return lax.ppermute(value, ('blk', 'ulysses'), pairs)]
where the time goes in v1:
time: 47.5 us; the launch traced here: 47.8 us
  starting transfers between devices  26.7 us (56%)
  waiting for transfers between devices  12.4 us (26%)
  Pallas kernels  7.28 us (15%)
  local copies, waits for them, and re-layouts  0.73 us (2%)
  between operations  0.73 us (2%)
    ppermute x12, starting transfers between devices, move(): return lax.ppermute(value, ('blk', 'ulysses'), pairs)  26.7 us
    ppermute x12, waiting for transfers between devices, move(): return lax.ppermute(value, ('blk', 'ulysses'), pairs)  12.4 us
    pallas_call x1, Pallas kernels, per_device(): pl.pallas_call(functools.partial(pack_kernel, n_mixed), out_shape=[unit]...  2.88 us
    pallas_call x1, Pallas kernels, per_device(): pl.pallas_call(functools.partial(pack_turns_kernel, side), out_shape=[uni...  1.32 us
    pallas_call x1, Pallas kernels, per_device(): pl.pallas_call(functools.partial(join_kernel, side), out_shape=[shape(tok...  0.97 us
  transfers between devices with their start and end apart: 12, of which 4 were waited for; matrix products, arithmetic and copies ran while one was open for 0% of the time, Pallas kernels for 10%

profile of v1, /device:TPU:1, one launch (start us, length us, event | category | flops | bytes accessed | tf_op | source)
XLA Modules:
  0.0 47.8 jit_solution(8783627484638834499)
XLA Ops:
  0.6 1.3 %pack_turns.1 = (bf16[128,512]{1,0:T(8,128)(2,1)S(1)}, bf16[128,512]{1,0:T(8,128)(2,1)S(1)}, bf16[128,512]{1,0:T(8,128)(2,1)S(1)}, bf16[128,512]{1,0:T(8,128)(2,1)S(1)}, f32[8,128]{1,0:T(8,128)S(1)}) custom-call(bf16[128,2048]{1,0:T(8,128)(2,1)} %q.7, bf16[128,2048]{1,0:T(8,128)(2,1)} %do.7, bf16[128,512]{1,0:T(8,128)(2,1)} %k.3, bf16[128,512]{1,0:T(8,128)(2,1)} %v.3), custom_call_target="tpu_custom_call" | custom-call | tf_op jit(solution)/shard_map/pack_turns/pallas_call | solution.py:419
  1.9 0.0 copy-start.3
  2.0 2.2 %collective-permute-start = (bf16[128,512]{1,0:T(8,128)(2,1)S(1)}, bf16[128,512]{1,0:T(8,128)(2,1)S(1)}, u32[]{:S(2)}, u32[]{:S(2)}) collective-permute-start(bf16[128,512]{1,0:T(8,128)(2,1)S(1)} %get-tuple-element.29), channel_id=1, source_target_pairs={{0,6},{1,7},{2,3},{3,2},{4,5},{5,4},{6,8},{7,9},{8,14},{9,15},{10,... | collective-permute-start | bytes 393224 | tf_op jit(solution)/shard_map/ppermute | solution.py:407
  4.1 0.1 collective-permute-start.1
  4.2 4.5 %collective-permute-start.2 = (bf16[128,512]{1,0:T(8,128)(2,1)S(1)}, bf16[128,512]{1,0:T(8,128)(2,1)S(1)}, u32[]{:S(2)}, u32[]{:S(2)}) collective-permute-start(bf16[128,512]{1,0:T(8,128)(2,1)S(1)} %get-tuple-element.31), channel_id=1, source_target_pairs={{0,1},{1,0},{2,4},{3,5},{4,10},{5,11},{6,7},{7,6},{8,9},{9,8},{10,... | collective-permute-start | bytes 393224 | tf_op jit(solution)/shard_map/ppermute | solution.py:407
  8.7 1.0 %collective-permute-start.3 = (bf16[128,512]{1,0:T(8,128)(2,1)S(1)}, bf16[128,512]{1,0:T(8,128)(2,1)S(1)}, u32[]{:S(2)}, u32[]{:S(2)}) collective-permute-start(bf16[128,512]{1,0:T(8,128)(2,1)S(1)} %get-tuple-element.32), channel_id=1, source_target_pairs={{0,1},{1,0},{2,5},{3,4},{4,11},{5,10},{6,7},{7,6},{8,9},{9,8},{10,... | collective-permute-start | bytes 393224 | tf_op jit(solution)/shard_map/ppermute | solution.py:407
  9.7 0.0 copy-done.3
  9.7 0.0 copy-start
  9.7 0.0 copy-start.1
  9.7 2.9 %pack.1 = (bf16[128,512]{1,0:T(8,128)(2,1)}, bf16[128,512]{1,0:T(8,128)(2,1)}, bf16[128,1152]{1,0:T(8,128)(2,1)}, f32[32,128]{1,0:T(8,128)}) custom-call(bf16[128,2048]{1,0:T(8,128)(2,1)} %q.7, bf16[128,2048]{1,0:T(8,128)(2,1)} %do.7, bf16[128,2048]{1,0:T(8,128)(2,1)} %o.1, f32[32,128]{1,0:T(8,128)} %bitcast.1, bf16[128,512]{1,0:T(8,128)(2,1)} %k.3, ...), custom_call_target="tpu_custom_call" | custom-call | tf_op jit(solution)/shard_map/pack/pallas_call | solution.py:427
  12.6 0.3 collective-permute-start.4
  12.9 0.0 collective-permute-done.rest_0_
  12.9 1.3 %collective-permute-start.5 = (bf16[128,512]{1,0:T(8,128)(2,1)}, bf16[128,512]{1,0:T(8,128)(2,1)S(1)}, u32[]{:S(2)}, u32[]{:S(2)}) collective-permute-start(bf16[128,512]{1,0:T(8,128)(2,1)} %get-tuple-element.39), channel_id=1, source_target_pairs={{0,4},{1,5},{2,6},{3,7},{4,8},{5,9},{6,10},{7,11},{8,12},{9,13},{1... | collective-permute-start | bytes 393224 | tf_op jit(solution)/shard_map/ppermute | solution.py:407
  14.2 0.0 collective-permute-done.1.rest_1_
  14.2 0.0 copy-start.4
  14.2 4.5 %collective-permute-start.6 = (bf16[128,512]{1,0:T(8,128)(2,1)}, bf16[128,512]{1,0:T(8,128)(2,1)S(1)}, u32[]{:S(2)}, u32[]{:S(2)}) collective-permute-start(bf16[128,512]{1,0:T(8,128)(2,1)} %get-tuple-element.40), channel_id=1, source_target_pairs={{0,5},{1,4},{2,7},{3,6},{4,9},{5,8},{6,11},{7,10},{8,13},{9,12},{1... | collective-permute-start | bytes 393224 | tf_op jit(solution)/shard_map/ppermute | solution.py:407
  18.7 0.0 collective-permute-done.2.rest_2_
  18.7 0.7 %collective-permute-done.3.rest_3_ = bf16[128,512]{1,0:T(8,128)(2,1)S(1)} collective-permute-done((bf16[128,512]{1,0:T(8,128)(2,1)S(1)}, bf16[128,512]{1,0:T(8,128)(2,1)S(1)}, u32[]{:S(2)}, u32[]{:S(2)}) %collective-permute-start.3) | collective-permute-done | bytes 131104 | tf_op jit(solution)/shard_map/ppermute | solution.py:407
  19.4 0.0 copy-done
  19.4 0.0 copy-done.1
  19.4 0.0 copy-done.4
  19.4 0.0 copy-start.2
  19.4 0.7 %copy-done.2 = f32[32,128]{1,0:T(8,128)S(1)} copy-done((f32[32,128]{1,0:T(8,128)S(1)}, f32[32,128]{1,0:T(8,128)}, u32[]{:S(2)}) %copy-start.2) | copy-done | bytes 16408
  20.1 0.6 %own_far.1 = (bf16[256,512]{1,0:T(8,128)(2,1)S(1)}, bf16[256,512]{1,0:T(8,128)(2,1)S(1)}, f32[256,512]{1,0:T(8,128)S(1)}, f32[1024,128]{1,0:T(8,128)S(1)}, s32[8,128]{1,0:T(8,128)S(1)}) custom-call(s32[16]{0:T(128)S(1)} %copy-done.4, bf16[128,2048]{1,0:T(8,128)(2,1)S(1)} %copy-done, bf16[128,2048]{1,0:T(8,128)(2,1)S(1)} %copy-done.1, ...), custom_call_target="tpu_custom_call" | custom-call | flops 2147483648 | bytes 1048576 | tf_op jit(solution)/shard_map/own_far/pallas_call | solution.py:447
  20.8 2.5 %collective-permute-done.4.rest = bf16[128,1152]{1,0:T(8,128)(2,1)S(1)} collective-permute-done((bf16[128,1152]{1,0:T(8,128)(2,1)}, bf16[128,1152]{1,0:T(8,128)(2,1)S(1)}, u32[]{:S(2)}, u32[]{:S(2)}) %collective-permute-start.4) | collective-permute-done | bytes 294944 | tf_op jit(solution)/shard_map/ppermute | solution.py:407
  23.3 0.4 far.1
  23.7 5.2 %collective-permute-start.7 = (bf16[128,512]{1,0:T(8,128)(2,1)S(1)}, bf16[128,512]{1,0:T(8,128)(2,1)S(1)}, u32[]{:S(2)}, u32[]{:S(2)}) collective-permute-start(bf16[128,512]{1,0:T(8,128)(2,1)S(1)} %get-tuple-element.46), channel_id=1, source_target_pairs={{0,30},{1,31},{2,28},{3,29},{4,2},{5,3},{6,0},{7,1},{8,6},{9,7},{1... | collective-permute-start | bytes 393224 | tf_op jit(solution)/shard_map/ppermute | solution.py:407
  28.9 0.0 collective-permute-done.5.refs_0_
  28.9 0.0 collective-permute-done.6.refs_1_
  28.9 0.4 near.1
  29.3 0.2 collective-permute-start.9
  29.5 5.4 %collective-permute-start.8 = (bf16[128,512]{1,0:T(8,128)(2,1)S(1)}, bf16[128,512]{1,0:T(8,128)(2,1)S(1)}, u32[]{:S(2)}, u32[]{:S(2)}) collective-permute-start(bf16[128,512]{1,0:T(8,128)(2,1)S(1)} %get-tuple-element.47), channel_id=1, source_target_pairs={{0,31},{1,30},{2,29},{3,28},{4,3},{5,2},{6,1},{7,0},{8,7},{9,6},{1... | collective-permute-start | bytes 393224 | tf_op jit(solution)/shard_map/ppermute | solution.py:407
  34.9 0.6 %own_near.1 = (bf16[128,512]{1,0:T(8,128)(2,1)S(1)}, bf16[128,512]{1,0:T(8,128)(2,1)S(1)}, bf16[128,1024]{1,0:T(8,128)(2,1)S(1)}) custom-call(s32[8,128]{1,0:T(8,128)S(1)} %get-tuple-element.33.flags, bf16[128,2048]{1,0:T(8,128)(2,1)S(1)} %copy-done, bf16[128,2048]{1,0:T(8,128)(2,1)S(1)} %copy-done.1, f32[32,128]{1,0:T(8,128)S(1)} %copy-done.2, ...), custom_call_target="tpu_custom_call" | custom-call | flops 1048576 | bytes 1048576 | tf_op jit(solution)/shard_map/own_near/pallas_call | solution.py:482
  35.5 0.1 collective-permute-start.10
  35.6 2.0 %collective-permute-start.11 = (bf16[128,512]{1,0:T(8,128)(2,1)S(1)}, bf16[128,512]{1,0:T(8,128)(2,1)S(1)}, u32[]{:S(2)}, u32[]{:S(2)}) collective-permute-start(bf16[128,512]{1,0:T(8,128)(2,1)S(1)} %get-tuple-element.50), channel_id=1, source_target_pairs={{0,28},{1,29},{2,30},{3,31},{4,0},{5,1},{6,2},{7,3},{8,4},{9,5},{1... | collective-permute-start | bytes 393224 | tf_op jit(solution)/shard_map/ppermute | solution.py:407
  37.6 0.0 collective-permute-done.7.refs_0_
  37.6 4.7 %collective-permute-done.8.refs_0_ = bf16[128,512]{1,0:T(8,128)(2,1)S(1)} collective-permute-done((bf16[128,512]{1,0:T(8,128)(2,1)S(1)}, bf16[128,512]{1,0:T(8,128)(2,1)S(1)}, u32[]{:S(2)}, u32[]{:S(2)}) %collective-permute-start.8) | collective-permute-done | bytes 131104 | tf_op jit(solution)/shard_map/ppermute | solution.py:407
  42.3 0.0 collective-permute-done.9.refs_0_
  42.3 4.5 %collective-permute-done.10.refs_3_ = bf16[128,512]{1,0:T(8,128)(2,1)S(1)} collective-permute-done((bf16[128,512]{1,0:T(8,128)(2,1)S(1)}, bf16[128,512]{1,0:T(8,128)(2,1)S(1)}, u32[]{:S(2)}, u32[]{:S(2)}) %collective-permute-start.10) | collective-permute-done | bytes 131104 | tf_op jit(solution)/shard_map/ppermute | solution.py:407
  46.9 0.0 collective-permute-done.11.refs_4_
  46.9 1.0 %join.1 = (bf16[128,2048]{1,0:T(8,128)(2,1)}, bf16[128,512]{1,0:T(8,128)(2,1)}, bf16[128,512]{1,0:T(8,128)(2,1)}) custom-call(bf16[128,1024]{1,0:T(8,128)(2,1)S(1)} %get-tuple-element.45.dq_own, f32[128,512]{1,0:T(8,128)S(1)} %take.3.refs_1_.refs_0_, f32[128,512]{1,0:T(8,128)S(1)} %take.4.refs_1_, bf16[128,1024]{1,0:T(8,128)(2,1)S(1)} %take.5.refs_2_, ...), custom_call_target="tpu_custom_call" | custom-call | tf_op jit(solution)/shard_map/join/pallas_call | solution.py:511
  (3 shorter events, 0.1 us)
Async XLA Ops:
  1.9 7.7 %copy-start.3 = (f32[8,128]{1,0:T(8,128)}, f32[8,128]{1,0:T(8,128)S(1)}, u32[]{:S(2)}) copy-start(f32[8,128]{1,0:T(8,128)S(1)} %get-tuple-element.27._) | copy-start | bytes 12292
  2.0 10.9 %collective-permute-start = (bf16[128,512]{1,0:T(8,128)(2,1)S(1)}, bf16[128,512]{1,0:T(8,128)(2,1)S(1)}, u32[]{:S(2)}, u32[]{:S(2)}) collective-permute-start(bf16[128,512]{1,0:T(8,128)(2,1)S(1)} %get-tuple-element.29), channel_id=1, source_target_pairs={{0,6},{1,7},{2,3},{3,2},{4,5},{5,4},{6,8},{7,9},{8,14},{9,15},{10,... | collective-permute-start | bytes 393224 | tf_op jit(solution)/shard_map/ppermute | solution.py:407
  4.1 10.0 %collective-permute-start.1 = (bf16[128,512]{1,0:T(8,128)(2,1)S(1)}, bf16[128,512]{1,0:T(8,128)(2,1)S(1)}, u32[]{:S(2)}, u32[]{:S(2)}) collective-permute-start(bf16[128,512]{1,0:T(8,128)(2,1)S(1)} %get-tuple-element.30), channel_id=1, source_target_pairs={{0,7},{1,6},{2,3},{3,2},{4,5},{5,4},{6,9},{7,8},{8,15},{9,14},{10,... | collective-permute-start | bytes 393224 | tf_op jit(solution)/shard_map/ppermute | solution.py:407
  4.2 14.5 %collective-permute-start.2 = (bf16[128,512]{1,0:T(8,128)(2,1)S(1)}, bf16[128,512]{1,0:T(8,128)(2,1)S(1)}, u32[]{:S(2)}, u32[]{:S(2)}) collective-permute-start(bf16[128,512]{1,0:T(8,128)(2,1)S(1)} %get-tuple-element.31), channel_id=1, source_target_pairs={{0,1},{1,0},{2,4},{3,5},{4,10},{5,11},{6,7},{7,6},{8,9},{9,8},{10,... | collective-permute-start | bytes 393224 | tf_op jit(solution)/shard_map/ppermute | solution.py:407
  8.7 10.7 %collective-permute-start.3 = (bf16[128,512]{1,0:T(8,128)(2,1)S(1)}, bf16[128,512]{1,0:T(8,128)(2,1)S(1)}, u32[]{:S(2)}, u32[]{:S(2)}) collective-permute-start(bf16[128,512]{1,0:T(8,128)(2,1)S(1)} %get-tuple-element.32), channel_id=1, source_target_pairs={{0,1},{1,0},{2,5},{3,4},{4,11},{5,10},{6,7},{7,6},{8,9},{9,8},{10,... | collective-permute-start | bytes 393224 | tf_op jit(solution)/shard_map/ppermute | solution.py:407
  9.7 9.7 %copy-start = (bf16[128,2048]{1,0:T(8,128)(2,1)S(1)}, bf16[128,2048]{1,0:T(8,128)(2,1)}, u32[]{:S(2)}) copy-start(bf16[128,2048]{1,0:T(8,128)(2,1)} %q.7) | copy-start | bytes 1572868
  9.7 9.7 %copy-start.1 = (bf16[128,2048]{1,0:T(8,128)(2,1)S(1)}, bf16[128,2048]{1,0:T(8,128)(2,1)}, u32[]{:S(2)}) copy-start(bf16[128,2048]{1,0:T(8,128)(2,1)} %do.7) | copy-start | bytes 1572868
  12.6 10.7 %collective-permute-start.4 = (bf16[128,1152]{1,0:T(8,128)(2,1)}, bf16[128,1152]{1,0:T(8,128)(2,1)S(1)}, u32[]{:S(2)}, u32[]{:S(2)}) collective-permute-start(bf16[128,1152]{1,0:T(8,128)(2,1)} %get-tuple-element.35), channel_id=1, source_target_pairs={{0,1},{1,0},{2,3},{3,2},{4,5},{5,4},{6,7},{7,6},{8,9},{9,8},{10,11... | collective-permute-start | bytes 884744 | tf_op jit(solution)/shard_map/ppermute | solution.py:407
  12.9 16.0 %collective-permute-start.5 = (bf16[128,512]{1,0:T(8,128)(2,1)}, bf16[128,512]{1,0:T(8,128)(2,1)S(1)}, u32[]{:S(2)}, u32[]{:S(2)}) collective-permute-start(bf16[128,512]{1,0:T(8,128)(2,1)} %get-tuple-element.39), channel_id=1, source_target_pairs={{0,4},{1,5},{2,6},{3,7},{4,8},{5,9},{6,10},{7,11},{8,12},{9,13},{1... | collective-permute-start | bytes 393224 | tf_op jit(solution)/shard_map/ppermute | solution.py:407
  14.2 5.2 %copy-start.4 = (s32[16]{0:T(128)S(1)}, s32[16]{0:T(128)}, u32[]{:S(2)}) copy-start(s32[16]{0:T(128)} %owners.1) | copy-start | bytes 196
  14.2 14.7 %collective-permute-start.6 = (bf16[128,512]{1,0:T(8,128)(2,1)}, bf16[128,512]{1,0:T(8,128)(2,1)S(1)}, u32[]{:S(2)}, u32[]{:S(2)}) collective-permute-start(bf16[128,512]{1,0:T(8,128)(2,1)} %get-tuple-element.40), channel_id=1, source_target_pairs={{0,5},{1,4},{2,7},{3,6},{4,9},{5,8},{6,11},{7,10},{8,13},{9,12},{1... | collective-permute-start | bytes 393224 | tf_op jit(solution)/shard_map/ppermute | solution.py:407
  19.4 0.7 %copy-start.2 = (f32[32,128]{1,0:T(8,128)S(1)}, f32[32,128]{1,0:T(8,128)}, u32[]{:S(2)}) copy-start(f32[32,128]{1,0:T(8,128)} %get-tuple-element.28.stats) | copy-start | bytes 49156
  23.7 13.9 %collective-permute-start.7 = (bf16[128,512]{1,0:T(8,128)(2,1)S(1)}, bf16[128,512]{1,0:T(8,128)(2,1)S(1)}, u32[]{:S(2)}, u32[]{:S(2)}) collective-permute-start(bf16[128,512]{1,0:T(8,128)(2,1)S(1)} %get-tuple-element.46), channel_id=1, source_target_pairs={{0,30},{1,31},{2,28},{3,29},{4,2},{5,3},{6,0},{7,1},{8,6},{9,7},{1... | collective-permute-start | bytes 393224 | tf_op jit(solution)/shard_map/ppermute | solution.py:407
  29.3 13.0 %collective-permute-start.9 = (bf16[128,1024]{1,0:T(8,128)(2,1)S(1)}, bf16[128,1024]{1,0:T(8,128)(2,1)S(1)}, u32[]{:S(2)}, u32[]{:S(2)}) collective-permute-start(bf16[128,1024]{1,0:T(8,128)(2,1)S(1)} %get-tuple-element.48), channel_id=1, source_target_pairs={{0,1},{1,0},{2,3},{3,2},{4,5},{5,4},{6,7},{7,6},{8,9},{9,8},{10,11... | collective-permute-start | bytes 786440 | tf_op jit(solution)/shard_map/ppermute | solution.py:407
  29.5 12.8 %collective-permute-start.8 = (bf16[128,512]{1,0:T(8,128)(2,1)S(1)}, bf16[128,512]{1,0:T(8,128)(2,1)S(1)}, u32[]{:S(2)}, u32[]{:S(2)}) collective-permute-start(bf16[128,512]{1,0:T(8,128)(2,1)S(1)} %get-tuple-element.47), channel_id=1, source_target_pairs={{0,31},{1,30},{2,29},{3,28},{4,3},{5,2},{6,1},{7,0},{8,7},{9,6},{1... | collective-permute-start | bytes 393224 | tf_op jit(solution)/shard_map/ppermute | solution.py:407
  35.5 11.3 %collective-permute-start.10 = (bf16[128,512]{1,0:T(8,128)(2,1)S(1)}, bf16[128,512]{1,0:T(8,128)(2,1)S(1)}, u32[]{:S(2)}, u32[]{:S(2)}) collective-permute-start(bf16[128,512]{1,0:T(8,128)(2,1)S(1)} %get-tuple-element.49), channel_id=1, source_target_pairs={{0,29},{1,28},{2,31},{3,30},{4,1},{5,0},{6,3},{7,2},{8,5},{9,4},{1... | collective-permute-start | bytes 393224 | tf_op jit(solution)/shard_map/ppermute | solution.py:407
  35.6 11.3 %collective-permute-start.11 = (bf16[128,512]{1,0:T(8,128)(2,1)S(1)}, bf16[128,512]{1,0:T(8,128)(2,1)S(1)}, u32[]{:S(2)}, u32[]{:S(2)}) collective-permute-start(bf16[128,512]{1,0:T(8,128)(2,1)S(1)} %get-tuple-element.50), channel_id=1, source_target_pairs={{0,28},{1,29},{2,30},{3,31},{4,0},{5,1},{6,2},{7,3},{8,4},{9,5},{1... | collective-permute-start | bytes 393224 | tf_op jit(solution)/shard_map/ppermute | solution.py:407
